TPU v7x, 256 devices: a whole 4x4x8 slice. The times are simulated.
256 devices in a mesh: ctx: 32 (over z, x), tp: 8 (over y, core).
Axes of the slice: x: 4, y: 4, z: 8, core: 2. Of those that a mesh axis runs over, the one named last changes fastest.
Arguments:
- hyena_in: bfloat16 [6144, 3, 8192], P('ctx', None, 'tp'), may hold values from -6 to 6
- stream_in: bfloat16 [6144, 8192], P('ctx', 'tp'), may hold values from -12 to 12
- feat_filter: float32 [3, 3, 8192], P(None, None, 'tp'), may hold values from -3 to 3
- inner_filter: float32 [7, 8192], P(None, 'tp'), may hold values from -2.5 to 2.5
- queries: bfloat16 [6144, 8192], P('ctx', 'tp'), may hold values from -10 to 10
- key_vectors: bfloat16 [6144, 8192], P('ctx', 'tp'), may hold values from -4.1 to 4.1
- segments: int32 [6144], replicated, may hold values from 0 to 63, as said below
Outputs:
- stream: bfloat16 [6144, 8192], P('ctx', 'tp')
- attended: bfloat16 [6144, 8192], P('ctx', 'tp')
Inputs may be any that keep to these rules, and one draw needn't show every extreme that they name: segments never fall; every document has 1 to 3072 tokens, and one has exactly 3072.
All inputs are finite; a program needn't handle non-finite values.
Results may differ from a plain program's by a relative error of at most 0.006.
Values may be sent and summed in bfloat16 or wider, within the bound.
A program may use at most 128 MiB of HBM per device.

v0:
```python
import math

import jax
import jax.numpy as jnp
from jax import lax
from jax.sharding import PartitionSpec as P

D = 8192
HEAD_DIM = 128


epsilon = 1e-05


def from_behind(value, axis, steps):
    count = lax.axis_size(axis)
    initial, last = (max(0, -steps), min(count, count - steps))
    return lax.ppermute(value, axis, [(source, source + steps) for source in range(initial, last)])


def apply_taps(series, segs, taps, out_rows):
    total_rows = series.shape[0]
    offset = total_rows - out_rows
    seg_here = segs[offset:]
    result = jnp.zeros((out_rows,) + series.shape[1:], series.dtype)
    for tap_index in range(taps.shape[0]):
        lower_row = offset - tap_index
        shifted = series[lower_row : lower_row + out_rows]
        same_doc = (segs[lower_row : lower_row + out_rows] == seg_here).astype(series.dtype)
        same_doc = same_doc.reshape((out_rows,) + (1,) * (series.ndim - 1))
        result = result + taps[tap_index] * shifted * same_doc
    return result


def body(hyena_in, stream_in, feat_filter, inner_filter, queries, key_vectors, segments):
    rows_here = hyena_in.shape[0]
    channels = hyena_in.shape[2]
    position = lax.axis_index("ctx")
    first_row = position * rows_here
    feat_taps = feat_filter.shape[0]
    inner_taps = inner_filter.shape[0]
    rim_depth = feat_taps - 1 + inner_taps - 1
    padded_seg = jnp.concatenate([jnp.full((rim_depth,), -1, jnp.int32), segments])
    seg_window = lax.dynamic_slice_in_dim(padded_seg, first_row, rows_here + rim_depth)
    own_rows = hyena_in.astype(jnp.float32)
    rim_rows = from_behind(hyena_in[rows_here - (feat_taps - 1) :], "ctx", 1)
    extended = jnp.concatenate([rim_rows.astype(jnp.float32), own_rows])
    featured = apply_taps(extended, seg_window[inner_taps - 1 :], feat_filter, rows_here)
    product = featured[:, 1] * featured[:, 2]
    product_edge = from_behind(product[rows_here - (inner_taps - 1) :], "ctx", 1)
    mixing = apply_taps(
        jnp.concatenate([product_edge, product]),
        seg_window[feat_taps - 1 :],
        inner_filter,
        rows_here,
    )
    stream = (stream_in.astype(jnp.float32) + featured[:, 0] * mixing).astype(jnp.bfloat16)
    widened = stream.astype(jnp.float32)
    row_total = lax.psum(jnp.sum(widened * widened, axis=1), "tp")
    norm_scale = lax.rsqrt(row_total / D + epsilon)
    values = (widened * norm_scale[:, None]).astype(jnp.bfloat16)
    heads_here = channels // HEAD_DIM
    inv_root = 1.0 / math.sqrt(HEAD_DIM)
    query_heads = queries.reshape(rows_here, heads_here, HEAD_DIM)
    seg_query = seg_window[rim_depth:]
    query_pos = first_row + jnp.arange(rows_here, dtype=jnp.int32)

    def fold_block(folded, key_block, value_block, key_start):
        key_count = key_block.shape[0]
        key_pos = key_start + jnp.arange(key_count, dtype=jnp.int32)
        seg_key = lax.dynamic_slice_in_dim(padded_seg, key_start + rim_depth, key_count)
        allowed = (
            (seg_query[:, None] == seg_key[None, :])
            & (key_pos[None, :] <= query_pos[:, None])
            & (key_pos[None, :] >= 0)
        )
        key_heads = key_block.reshape(key_count, heads_here, HEAD_DIM)
        value_heads = value_block.reshape(key_count, heads_here, HEAD_DIM)
        running, totals, accumulated = folded
        scores = (
            jnp.einsum("qhd,khd->qhk", query_heads, key_heads, preferred_element_type=jnp.float32)
            * inv_root
        )
        allowed_heads = allowed[:, None, :]
        masked = jnp.where(allowed_heads, scores, -1e30)
        new_top = jnp.maximum(running, jnp.max(masked, axis=2))
        factor = jnp.exp(running - new_top)
        exp_terms = jnp.where(allowed_heads, jnp.exp(scores - new_top[:, :, None]), 0.0)
        totals = totals * factor + jnp.sum(exp_terms, axis=2)
        accumulated = accumulated * factor[:, :, None] + jnp.einsum(
            "qhk,khd->qhd",
            exp_terms.astype(jnp.bfloat16),
            value_heads,
            preferred_element_type=jnp.float32,
        )
        return (new_top, totals, accumulated)

    initial = (
        jnp.full((rows_here, heads_here), -1e30, jnp.float32),
        jnp.zeros((rows_here, heads_here), jnp.float32),
        jnp.zeros((rows_here, heads_here, HEAD_DIM), jnp.float32),
    )
    key_part = lax.all_gather(key_vectors, "ctx", axis=0, tiled=True)
    value_part = lax.all_gather(values, "ctx", axis=0, tiled=True)
    key_count = key_part.shape[0]

    def block_turn(block_index, carried):
        block_start = block_index * 512
        key_block = lax.dynamic_slice_in_dim(key_part, block_start, 512)
        value_block = lax.dynamic_slice_in_dim(value_part, block_start, 512)
        return fold_block(carried, key_block, value_block, block_start)

    folded = lax.fori_loop(0, key_count // 512, block_turn, initial)
    running, totals, accumulated = folded
    attended = (accumulated / totals[:, :, None]).astype(jnp.bfloat16).reshape(rows_here, channels)
    return (stream, attended)


def solution(mesh):
    in_specs = (
        P("ctx", None, "tp"),
        P("ctx", "tp"),
        P(None, None, "tp"),
        P(None, "tp"),
        P("ctx", "tp"),
        P("ctx", "tp"),
        P(),
    )
    out_specs = (P("ctx", "tp"), P("ctx", "tp"))
    return jax.shard_map(body, mesh=mesh, in_specs=in_specs, out_specs=out_specs, check_vma=False)
```

profile of v0, /device:TPU:8, one launch (start us, length us, event | category | flops | bytes accessed | tf_op | source)
XLA Modules:
  0.0 382.1 jit_solution(17427376625662950626)
XLA Ops:
  8.8 3.4 collective-permute-start
  14.9 1.6 convert_element_type.58
  17.5 3.4 collective-permute-start.1
  21.1 1.5 collective-permute-done.1
  22.5 1.3 fusion.29
  23.8 10.7 %psum.7 = f32[192]{0:T(256)S(1)} all-reduce(f32[192]{0:T(256)S(1)} %get-tuple-element.325), channel_id=1, replica_groups=mesh['ctx'=32,'tp'=8] {'tp'}, use_global_device_ids=true, to_apply=%region_1.0 | all-reduce | flops 192 | bytes 1536 | tf_op jit(solution)/shard_map/psum | solution.py:59
  37.6 95.6 %all-gather.3.cloned.1.call-done = bf16[6144,1024]{1,0:T(8,128)(2,1)} async-done(((bf16[192,1024]{1,0:T(8,128)(2,1)}), bf16[6144,1024]{1,0:T(8,128)(2,1)}) %all-gather.3.cloned.1.call-update) | async-done | bytes 12582928 | tf_op jit(solution)/shard_map/all_gather | solution.py:103
  133.1 119.3 %all-gather.5.cloned.1.call-done = bf16[6144,1024]{1,0:T(8,128)(2,1)} async-done(((bf16[192,1024]{1,0:T(8,128)(2,1)}), bf16[6144,1024]{1,0:T(8,128)(2,1)}) %all-gather.5.cloned.1.call-update) | async-done | bytes 12582928 | tf_op jit(solution)/shard_map/all_gather | solution.py:104
  252.5 120.6 %while.20 = (s32[]{:T(128)}, f32[192,8]{0,1:T(8,128)S(1)}, f32[192,8]{0,1:T(8,128)S(1)}, f32[192,8,128]{2,0,1:T(8,128)}, s32[192]{0:T(256)}, /*index=5*/s32[6152...) while((s32[]{:T(128)}, f32[192,8]{0,1:T(8,128)S(1)}, ...), condition=%wide.region_5.6_spmd.clone, body=%wide.region_2.5_spmd.clone.sunk | while | flops 412296384 | bytes 29079148 | solution.py:113
  253.3 1.4 and_and_fusion.2
  254.7 1.7 constant_dynamic-slice_fusion.3
  257.5 1.8 fusion.78
  263.3 1.4 and_and_fusion.2
  264.8 1.7 constant_dynamic-slice_fusion.3
  267.6 1.8 fusion.78
  273.4 1.4 and_and_fusion.2
  274.8 1.7 constant_dynamic-slice_fusion.3
  277.6 1.8 fusion.78
  283.4 1.4 and_and_fusion.2
  284.9 1.7 constant_dynamic-slice_fusion.3
  287.7 1.8 fusion.78
  293.5 1.4 and_and_fusion.2
  294.9 1.7 constant_dynamic-slice_fusion.3
  297.8 1.8 fusion.78
  303.6 1.4 and_and_fusion.2
  305.0 1.7 constant_dynamic-slice_fusion.3
  307.8 1.8 fusion.78
  310.8 1.1 fusion.81
  313.6 1.4 and_and_fusion.2
  315.0 1.7 constant_dynamic-slice_fusion.3
  317.9 1.8 fusion.78
  323.7 1.4 and_and_fusion.2
  325.1 1.7 constant_dynamic-slice_fusion.3
  327.9 1.8 fusion.78
  333.7 1.4 and_and_fusion.2
  335.1 1.7 constant_dynamic-slice_fusion.3
  338.0 1.8 fusion.78
  343.8 1.4 and_and_fusion.2
  345.2 1.7 constant_dynamic-slice_fusion.3
  348.0 1.8 fusion.78
  353.8 1.4 and_and_fusion.2
  355.3 1.7 constant_dynamic-slice_fusion.3
  358.1 1.8 fusion.78
  363.9 1.4 and_and_fusion.2
  365.3 1.7 constant_dynamic-slice_fusion.3
  368.1 1.8 fusion.78
  371.1 1.1 fusion.81
  373.1 2.2 copy_bitcast_fusion
  (233 shorter events, 66.3 us)
Async XLA Ops:
  7.2 29.6 %copy-start = (bf16[192,1024]{1,0:T(8,128)(2,1)S(1)}, bf16[192,1024]{1,0:T(8,128)(2,1)}, u32[]{:S(2)}) copy-start(bf16[192,1024]{1,0:T(8,128)(2,1)} %param.13) | copy-start | bytes 1179652
  7.2 126.0 %all-gather.3.cloned.1.call-start = ((), (), s32[]{:S(2)}) async-start(), calls=%async_computation | async-start | bytes 12976128 | tf_op jit(solution)/shard_map/all_gather | solution.py:103
  7.9 244.6 %all-gather.5.cloned.1.call-start = ((), (), s32[]{:S(2)}) async-start(), calls=%async_computation.1 | async-start | bytes 12976128 | tf_op jit(solution)/shard_map/all_gather | solution.py:104
  8.8 7.7 %collective-permute-start = (bf16[2,3,1024]{2,0,1:T(2,128)(2,1)S(1)}, bf16[2,3,1024]{2,0,1:T(2,128)(2,1)S(1)}, u32[]{:S(2)}, u32[]{:S(2)}) collective-permute-start(bf16[2,3,1024]{2,0,1:T(2,128)(2,1)S(1)} %slice.113), channel_id=1, source_target_pairs={{0,8},{8,16},{16,24},{24,32},{32,40},{40,48},{48,56},{56,64},{64,7... | collective-permute-start | bytes 36872 | tf_op jit(solution)/shard_map/ppermute | solution.py:18
  17.4 5.1 %copy-start.5 = (bf16[192,1024]{1,0:T(8,128)(2,1)S(1)}, bf16[192,1024]{1,0:T(8,128)(2,1)}, u32[]{:S(2)}) copy-start(bf16[192,1024]{1,0:T(8,128)(2,1)} %param.10) | copy-start | bytes 1179652
  17.5 18.5 %copy-start.6 = (s32[6144]{0:T(1024)S(1)}, s32[6144]{0:T(1024)}, u32[]{:S(2)}) copy-start(s32[6144]{0:T(1024)} %param.15) | copy-start | bytes 73732
  17.5 5.0 %collective-permute-start.1 = (f32[6,1024]{1,0:T(8,128)S(1)}, f32[6,1024]{1,0:T(8,128)S(1)}, u32[]{:S(2)}, u32[]{:S(2)}) collective-permute-start(f32[6,1024]{1,0:T(8,128)S(1)} %slice_bitcast_fusion.1), channel_id=1, source_target_pairs={{0,8},{8,16},{16,24},{24,32},{32,40},{40,48},{48,56},{56,64},{64,7... | collective-permute-start | bytes 73736 | tf_op jit(solution)/shard_map/ppermute | solution.py:18
  23.8 228.7 %copy-start.2 = (bf16[192,1024]{1,0:T(8,128)(2,1)}, bf16[192,1024]{1,0:T(8,128)(2,1)S(1)}, u32[]{:S(2)}) copy-start(bf16[192,1024]{1,0:T(8,128)(2,1)S(1)} %get-tuple-element.326) | copy-start | bytes 1179652
  257.5 1.9 copy-start.1
  259.4 1.1 copy-start.3
  261.6 1.0 copy-start.4
  267.6 1.9 copy-start.1
  269.4 1.1 copy-start.3
  271.6 1.0 copy-start.4
  277.6 1.9 copy-start.1
  279.5 1.1 copy-start.3
  281.7 1.0 copy-start.4
  287.7 1.9 copy-start.1
  289.5 1.1 copy-start.3
  291.7 1.0 copy-start.4
  297.7 1.9 copy-start.1
  299.6 1.1 copy-start.3
  301.8 1.0 copy-start.4
  307.8 1.9 copy-start.1
  309.6 1.1 copy-start.3
  311.9 1.0 copy-start.4
  317.9 1.9 copy-start.1
  319.7 1.1 copy-start.3
  321.9 1.0 copy-start.4
  327.9 1.9 copy-start.1
  329.7 1.1 copy-start.3
  332.0 1.0 copy-start.4
  338.0 1.9 copy-start.1
  339.8 1.1 copy-start.3
  342.0 1.0 copy-start.4
  348.0 1.9 copy-start.1
  349.9 1.1 copy-start.3
  352.1 1.0 copy-start.4
  358.1 1.9 copy-start.1
  359.9 1.1 copy-start.3
  362.1 1.0 copy-start.4
  368.1 1.9 copy-start.1
  370.0 1.1 copy-start.3
  372.2 1.0 copy-start.4
Sparse Core Ops, SparseCore 0:
  10.6 122.5 all-gather.2
  135.7 116.7 all-gather.4
where the time goes:
time: 385 us; the launch traced here: 382 us
  waiting for transfers between devices  217 us (56%)
  local copies, waits for them, and re-layouts  60.5 us (16%)
  other arithmetic  36.8 us (10%)
  matrix products  34.8 us (9%)
  between operations  14.2 us (4%)
  blocking collectives  10.7 us (3%)
  starting transfers between devices  6.88 us (2%)
    all_gather x1, waiting for transfers between devices, body(): value_part = lax.all_gather(values, 'ctx', axis=0, tiled=True)  119 us
    all_gather x1, waiting for transfers between devices, body(): key_part = lax.all_gather(key_vectors, 'ctx', axis=0, tiled=True)  95.6 us
    dynamic_slice x24, local copies, waits for them, and re-layouts, block_turn(): value_block = lax.dynamic_slice_in_dim(value_part, block_start, 512)  27.1 us
    dot_general x12, matrix products, fold_block(): jnp.einsum('qhd,khd->qhk', query_heads, key_heads, preferred_element_type...  21.9 us
    and x12, other arithmetic, fold_block(): (seg_query[:, None] == seg_key[None, :]) & (key_pos[None, :] <= query_pos...  17 us
    dot_general x12, matrix products, fold_block(): jnp.einsum('qhk,khd->qhd', exp_terms.astype(jnp.bfloat16), value_heads, p...  12.9 us
    reduce_sum x12, other arithmetic, fold_block(): totals = totals * factor + jnp.sum(exp_terms, axis=2)  12.3 us
    while x84, local copies, waits for them, and re-layouts  12.1 us
  transfers between devices with their start and end apart: 4, of which 3 were waited for; matrix products, arithmetic and copies ran while one was open for 3% of the time, Pallas kernels for 0%

commit v1 on v0

v1 whole, which is shorter than its diff:
```python
import functools
import math

import jax
import jax.numpy as jnp
from jax import lax
from jax.experimental import pallas as pl
from jax.experimental.pallas import tpu as pltpu
from jax.sharding import PartitionSpec as P

HEAD_DIM = 128
HALO = 16
EPSILON = 1e-05
BIG = 1e30
MESH = pl.DeviceIdType.MESH
F32 = jnp.float32
BF16 = jnp.bfloat16
RING_X = 4


def ring_offsets(count):
    offsets = [0]
    for distance in range(1, count // 2 + 1):
        offsets.append(distance)
        if distance != count - distance:
            offsets.append(-distance)
    return offsets


def slot_of(delta, count):
    ahead = jnp.maximum(2 * delta - 1, 0)
    return jnp.where(delta <= count // 2, ahead, 2 * (count - delta))


def front_kernel(
    ring_z, ring_tp, rows,
    hyena, stream_in, feat, inner, queries, keys, seg,
    stream_out, q_all, k_all, v_all,
    hyena_buf, wide, product, gate_free, stream_buf, values, segcol, sums, total_col, in_buf,
    load_sem, own_sem, halo_sem, sum_send, sum_recv,
    z_send, z_recv, x_send, x_recv, far_send, far_recv,
):
    ctx = lax.axis_index("ctx")
    tp = lax.axis_index("tp")
    z = ctx // RING_X
    x = ctx % RING_X
    ring_ctx = ring_z * RING_X
    channels = queries.shape[1]
    offsets = ring_offsets(ring_z)
    half = rows // 2
    right = (x + 1) % RING_X
    left = (x + RING_X - 1) % RING_X
    far = (x + 2) % RING_X
    right_id = (z * RING_X + right, tp)
    left_id = (z * RING_X + left, tp)
    next_ctx = (ctx + 1) % ring_ctx
    prev_ctx = (ctx + ring_ctx - 1) % ring_ctx

    def z_at(offset):
        return (z + offset + ring_z) % ring_z

    def head_cols(index):
        return pl.ds(pl.multiple_of(index * HEAD_DIM, HEAD_DIM), HEAD_DIM)

    load_h = pltpu.make_async_copy(hyena, hyena_buf.at[:, pl.ds(HALO, rows)], load_sem.at[0])
    load_s = pltpu.make_async_copy(stream_in, in_buf, load_sem.at[1])
    load_h.start()
    load_s.start()
    own_k = pltpu.make_async_copy(keys.at[:, head_cols(z)], k_all.at[0, x], own_sem.at[0])
    own_q = pltpu.make_async_copy(queries.at[:, head_cols(z)], q_all.at[0], own_sem.at[1])
    own_k.start()
    own_q.start()

    barrier = pltpu.get_barrier_semaphore()
    partners = [(z_at(offset) * RING_X + x, tp) for offset in offsets[1:]]
    partners += [right_id, left_id, (next_ctx, tp), (prev_ctx, tp)]
    partners += [(ctx, (tp + step) % ring_tp) for step in range(1, ring_tp)]
    for partner in partners:
        pl.semaphore_signal(barrier, inc=1, device_id=partner, device_id_type=MESH)

    def seg_row(row, carry):
        token = ctx * rows - HALO + row
        number = jnp.where(token >= 0, seg[jnp.maximum(token, 0)], -1)
        segcol[pl.ds(row, 1), :] = jnp.full((1, 128), number, jnp.int32)
        return carry

    lax.fori_loop(0, HALO + rows, seg_row, 0)

    pl.semaphore_wait(barrier, len(partners))

    halo = pltpu.make_async_remote_copy(
        src_ref=hyena.at[:, pl.ds(rows - HALO, HALO)],
        dst_ref=hyena_buf.at[:, pl.ds(0, HALO)],
        send_sem=halo_sem.at[0], recv_sem=halo_sem.at[1],
        device_id=(next_ctx, tp), device_id_type=MESH,
    )
    halo.start()

    def z_copy(kind, slot, source, target):
        goal = z_at(-offsets[slot])
        return pltpu.make_async_remote_copy(
            src_ref=source.at[:, head_cols(goal)], dst_ref=target,
            send_sem=z_send.at[kind, slot], recv_sem=z_recv.at[kind, slot],
            device_id=(goal * RING_X + x, tp), device_id_type=MESH,
        )

    k_copies = [z_copy(0, slot, keys, k_all.at[slot, x]) for slot in range(1, ring_z)]
    for copy in k_copies:
        copy.start()

    load_h.wait()
    load_s.wait()
    wide[:, pl.ds(HALO, rows)] = hyena_buf[:, pl.ds(HALO, rows)].astype(F32)
    halo.wait_recv()
    wide[:, pl.ds(0, HALO)] = hyena_buf[:, pl.ds(0, HALO)].astype(F32)
    feat_taps, inner_taps = feat.shape[0], inner.shape[0]

    def tile_lanes(mask):
        return jnp.concatenate([mask] * (channels // 128), axis=1)

    def featured(group, start, count, masks):
        result = None
        for tap in range(feat_taps):
            term = feat[tap, group][None, :] * wide[group, pl.ds(start - tap, count), :]
            if tap > 0:
                term = term * masks[tap]
            result = term if result is None else result + term
        return result

    def masks_of(start, count, taps):
        here = segcol[pl.ds(start, count), :]
        return [None] + [
            tile_lanes((segcol[pl.ds(start - tap, count), :] == here).astype(F32))
            for tap in range(1, taps)
        ]

    masks = masks_of(8, 8, feat_taps)
    product[pl.ds(8, 8), :] = featured(1, 8, 8, masks) * featured(2, 8, 8, masks)

    for start in range(HALO, HALO + rows, 8):
        masks = masks_of(start, 8, inner_taps)
        key_value = featured(1, start, 8, masks) * featured(2, start, 8, masks)
        product[pl.ds(start, 8), :] = key_value
        mixing = inner[0][None, :] * key_value
        for tap in range(1, inner_taps):
            mixing = mixing + inner[tap][None, :] * product[pl.ds(start - tap, 8), :] * masks[tap]
        gate_free[pl.ds(start - HALO, 8), :] = featured(0, start, 8, masks) * mixing

    for start in range(0, rows, 16):
        stream = (in_buf[pl.ds(start, 16), :].astype(F32) + gate_free[pl.ds(start, 16), :]).astype(BF16)
        stream_buf[pl.ds(start, 16), :] = stream
        stream = stream.astype(F32)
        square = stream * stream
        folded = square[:, 0:128]
        for lane in range(128, channels, 128):
            folded = folded + square[:, lane:lane + 128]
        total_col[pl.ds(start, 16), :] = folded
    store_s = pltpu.make_async_copy(stream_buf, stream_out, load_sem.at[0])
    store_s.start()

    padded = total_col.shape[0]
    if padded > rows:
        total_col[pl.ds(rows, padded - rows), :] = jnp.zeros((padded - rows, 128), F32)
    for start in range(0, padded, 128):
        turned = total_col[pl.ds(start, 128), :].T
        row = jnp.sum(turned, axis=0, keepdims=True)
        sums[tp, :, pl.ds(start, 128)] = jnp.broadcast_to(row, (8, 128))
    sum_copies = []
    for step in range(1, ring_tp):
        copy = pltpu.make_async_remote_copy(
            src_ref=sums.at[tp], dst_ref=sums.at[tp],
            send_sem=sum_send.at[step], recv_sem=sum_recv.at[step],
            device_id=(ctx, (tp + step) % ring_tp), device_id_type=MESH,
        )
        copy.start()
        sum_copies.append(copy)

    groups = [(0, 1)] + [(lo, min(lo + 2, ring_z)) for lo in range(1, ring_z, 2)]

    def near_copy(kind, group, way, array):
        lo, hi = groups[group]
        return pltpu.make_async_remote_copy(
            src_ref=array.at[pl.ds(lo, hi - lo), x], dst_ref=array.at[pl.ds(lo, hi - lo), x],
            send_sem=x_send.at[kind, group, way], recv_sem=x_recv.at[kind, group, way],
            device_id=(right_id, left_id)[way], device_id_type=MESH,
        )

    def near_wait(kind, group, way, array):
        lo, hi = groups[group]
        source = (left, right)[way]
        pltpu.make_async_remote_copy(
            src_ref=array.at[pl.ds(lo, hi - lo), source], dst_ref=array.at[pl.ds(lo, hi - lo), source],
            send_sem=x_send.at[kind, group, way], recv_sem=x_recv.at[kind, group, way],
            device_id=(right_id, left_id)[way], device_id_type=MESH,
        ).wait_recv()

    def far_copy(kind, group, way, array):
        lo, hi = groups[group]
        source = (left, right)[way]
        view = array.at[pl.ds(lo, hi - lo), source, pl.ds(way * half, half)]
        return pltpu.make_async_remote_copy(
            src_ref=view, dst_ref=view,
            send_sem=far_send.at[kind, group, way], recv_sem=far_recv.at[kind, group, way],
            device_id=(right_id, left_id)[way], device_id_type=MESH,
        )

    def far_wait(kind, group, way, array):
        lo, hi = groups[group]
        view = array.at[pl.ds(lo, hi - lo), far, pl.ds(way * half, half)]
        pltpu.make_async_remote_copy(
            src_ref=view, dst_ref=view,
            send_sem=far_send.at[kind, group, way], recv_sem=far_recv.at[kind, group, way],
            device_id=(right_id, left_id)[way], device_id_type=MESH,
        ).wait_recv()

    x_copies = []

    def first_hops(kind, array, z_copies, own):
        for group, (lo, hi) in enumerate(groups):
            if lo == 0:
                own.wait()
            else:
                for slot in range(lo, hi):
                    z_copies[slot - 1].wait_recv()
            for way in range(2):
                copy = near_copy(kind, group, way, array)
                copy.start()
                x_copies.append(copy)

    def second_hops(kind, array):
        for group in range(len(groups)):
            for way in range(2):
                near_wait(kind, group, way, array)
                copy = far_copy(kind, group, way, array)
                copy.start()
                x_copies.append(copy)

    first_hops(0, k_all, k_copies, own_k)

    total = sums[tp]
    for step in range(1, ring_tp):
        sum_copies[step - 1].wait_recv()
    for step in range(1, ring_tp):
        total = total + sums[(tp + step) % ring_tp]
    scale = lax.rsqrt(total / (channels * ring_tp) + EPSILON)
    for start in range(0, padded, 128):
        row = jnp.broadcast_to(scale[0:1, start:start + 128], (128, 128))
        total_col[pl.ds(start, 128), :] = row.T
    for start in range(0, rows, 16):
        norm = tile_lanes(total_col[pl.ds(start, 16), :])
        values[pl.ds(start, 16), :] = (stream_buf[pl.ds(start, 16), :].astype(F32) * norm).astype(BF16)

    v_copies = [z_copy(1, slot, values, v_all.at[slot, x]) for slot in range(1, ring_z)]
    for copy in v_copies:
        copy.start()
    own_v = pltpu.make_async_copy(values.at[:, head_cols(z)], v_all.at[0, x], own_sem.at[2])
    own_v.start()
    q_copies = [z_copy(2, slot, queries, q_all.at[slot]) for slot in range(1, ring_z)]
    for copy in q_copies:
        copy.start()

    second_hops(0, k_all)
    first_hops(1, v_all, v_copies, own_v)
    second_hops(1, v_all)
    own_q.wait()
    store_s.wait()
    for copy in q_copies:
        copy.wait_recv()
    for kind, array in ((0, k_all), (1, v_all)):
        for group in range(len(groups)):
            for way in range(2):
                far_wait(kind, group, way, array)
    halo.wait_send()
    for copy in sum_copies + k_copies + v_copies + q_copies + x_copies:
        copy.wait_send()


def attend_kernel(ring_z, tile_rows, seg, seg_lanes, q_all, k_all, v_all, out, scores_buf):
    ctx = lax.axis_index("ctx")
    z = ctx // RING_X
    x = ctx % RING_X
    rows = q_all.shape[1]
    tile = tile_rows
    per_z = RING_X * rows // tile
    blocks = tile // rows
    factor = math.log2(math.e) / math.sqrt(HEAD_DIM)
    last_token = seg.shape[0]
    steps = max(1, last_token.bit_length())
    lane_rows = tile // 128

    def key_tile(array, index):
        row_z = index // per_z
        slot = slot_of((row_z - z + ring_z) % ring_z, ring_z)
        part = index % per_z
        return array[slot, pl.ds(part * blocks, blocks)].reshape(tile, HEAD_DIM)

    def documents(index):
        return jnp.concatenate(
            [seg_lanes[pl.ds(index * lane_rows + i, 1), :] for i in range(lane_rows)], axis=1
        )

    numbers = lax.broadcasted_iota(jnp.int32, (128, tile), 0)

    for row_z in range(ring_z):
        block = row_z * RING_X + x
        first = block * rows
        slot = slot_of((row_z - z + ring_z) % ring_z, ring_z)
        first_doc = seg[first]
        last_doc = seg[first + rows - 1]

        def search(_, bounds):
            low, high = bounds
            mid = (low + high) // 2
            before = (seg[jnp.minimum(mid, last_token - 1)] < first_doc) & (low < high)
            return jnp.where(before, mid + 1, low), jnp.where(before | (low >= high), high, mid)

        low, _ = lax.fori_loop(0, steps, search, (0, first))
        lo_tile = low // tile
        hi_tile = first // tile
        q = q_all[slot]
        hits = (numbers == documents(hi_tile)).astype(F32)
        in_tile = first - hi_tile * tile

        q_docs = lax.cond(
            in_tile == 0,
            lambda: hits[:, 0:rows],
            lambda: hits[:, tile - rows:tile],
        )
        q_miss = (1.0 - q_docs).T.astype(BF16)

        def raw_scores(index):
            return lax.dot_general(
                q, key_tile(k_all, index), (((1,), (1,)), ((), ())), preferred_element_type=F32
            )

        def penalty(index):
            k_docs = jnp.where(numbers == documents(index), -BIG, 0.0).astype(BF16)
            return jnp.dot(q_miss, k_docs, preferred_element_type=F32)

        def fold_max(top, scores):
            for lane in range(0, tile, 128):
                top = jnp.maximum(top, scores[:, lane:lane + 128])
            return top

        def score_tile(index, top):
            scores = lax.cond(
                seg[index * tile] != last_doc,
                lambda: raw_scores(index) + penalty(index),
                lambda: raw_scores(index),
            )
            scores_buf[index - lo_tile] = scores
            return fold_max(top, scores)

        top = lax.fori_loop(lo_tile, hi_tile, score_tile, jnp.full((rows, 128), -BIG, F32))
        scores = raw_scores(hi_tile) + penalty(hi_tile)
        row_at = in_tile + lax.broadcasted_iota(jnp.int32, (rows, tile), 0)
        col_at = lax.broadcasted_iota(jnp.int32, (rows, tile), 1)
        scores = jnp.where(col_at <= row_at, scores, -BIG)
        scores_buf[hi_tile - lo_tile] = scores
        top = jnp.max(fold_max(top, scores), axis=1, keepdims=True)

        def weigh_tile(index, carry):
            sums, summed = carry
            terms = jnp.exp2((scores_buf[index - lo_tile] - top) * factor)
            for lane in range(0, tile, 128):
                sums = sums + terms[:, lane:lane + 128]
            summed = summed + jnp.dot(
                terms.astype(BF16), key_tile(v_all, index), preferred_element_type=F32
            )
            return sums, summed

        sums, summed = lax.fori_loop(
            lo_tile, hi_tile + 1, weigh_tile,
            (jnp.zeros((rows, 128), F32), jnp.zeros((rows, HEAD_DIM), F32)),
        )
        out[slot] = (summed / jnp.sum(sums, axis=1, keepdims=True)).astype(BF16)


def return_kernel(ring_z, results, attended, own_sem, send_sem, recv_sem):
    ctx = lax.axis_index("ctx")
    tp = lax.axis_index("tp")
    z = ctx // RING_X
    x = ctx % RING_X
    offsets = ring_offsets(ring_z)

    def z_at(offset):
        return (z + offset + ring_z) % ring_z

    def head_cols(index):
        return pl.ds(pl.multiple_of(index * HEAD_DIM, HEAD_DIM), HEAD_DIM)

    own = pltpu.make_async_copy(results.at[0], attended.at[:, head_cols(z)], own_sem)
    own.start()
    barrier = pltpu.get_barrier_semaphore()
    partners = [(z_at(offset) * RING_X + x, tp) for offset in offsets[1:]]
    for partner in partners:
        pl.semaphore_signal(barrier, inc=1, device_id=partner, device_id_type=MESH)
    pl.semaphore_wait(barrier, len(partners))
    copies = []
    for slot in range(1, ring_z):
        copy = pltpu.make_async_remote_copy(
            src_ref=results.at[slot], dst_ref=attended.at[:, head_cols(z)],
            send_sem=send_sem.at[slot], recv_sem=recv_sem.at[slot],
            device_id=(z_at(offsets[slot]) * RING_X + x, tp), device_id_type=MESH,
        )
        copy.start()
        copies.append(copy)
    own.wait()
    for slot in range(1, ring_z):
        view = attended.at[:, head_cols(z_at(-offsets[slot]))]
        pltpu.make_async_remote_copy(
            src_ref=results.at[slot], dst_ref=view,
            send_sem=send_sem.at[slot], recv_sem=recv_sem.at[slot],
            device_id=(z_at(offsets[slot]) * RING_X + x, tp), device_id_type=MESH,
        ).wait_recv()
    for copy in copies:
        copy.wait_send()


ANY = pl.BlockSpec(memory_space=pl.ANY)
VMEM = pl.BlockSpec(memory_space=pltpu.VMEM)
SMEM = pl.BlockSpec(memory_space=pltpu.SMEM)


def body(ring_ctx, ring_tp, most, hyena_in, stream_in, feat_filter, inner_filter, queries, key_vectors, segments):
    rows, channels = stream_in.shape
    ring_z = ring_ctx // RING_X
    tokens = segments.shape[0]
    hyena = jnp.transpose(hyena_in, (1, 0, 2))
    padded = -(-rows // 128) * 128
    dma = pltpu.SemaphoreType.DMA
    gathered = jax.ShapeDtypeStruct((ring_z, RING_X, rows, HEAD_DIM), BF16)
    group_count = 1 + ring_z // 2
    stream, q_all, k_all, v_all = pl.pallas_call(
        functools.partial(front_kernel, ring_z, ring_tp, rows),
        name="front",
        out_shape=(
            jax.ShapeDtypeStruct((rows, channels), BF16),
            jax.ShapeDtypeStruct((ring_z, rows, HEAD_DIM), BF16),
            gathered,
            gathered,
        ),
        in_specs=[ANY, ANY, VMEM, VMEM, ANY, ANY, SMEM],
        out_specs=(ANY, ANY, ANY, ANY),
        scratch_shapes=[
            pltpu.VMEM((3, HALO + rows, channels), BF16),
            pltpu.VMEM((3, HALO + rows, channels), F32),
            pltpu.VMEM((HALO + rows, channels), F32),
            pltpu.VMEM((rows, channels), F32),
            pltpu.VMEM((rows, channels), BF16),
            pltpu.VMEM((rows, channels), BF16),
            pltpu.VMEM((HALO + rows, 128), jnp.int32),
            pltpu.VMEM((ring_tp, 8, padded), F32),
            pltpu.VMEM((padded, 128), F32),
            pltpu.VMEM((rows, channels), BF16),
            dma((2,)), dma((3,)), dma((2,)), dma((ring_tp,)), dma((ring_tp,)),
            dma((3, ring_z)), dma((3, ring_z)),
            dma((2, group_count, 2)), dma((2, group_count, 2)),
            dma((2, group_count, 2)), dma((2, group_count, 2)),
        ],
        compiler_params=pltpu.CompilerParams(
            collective_id=0, has_side_effects=True, vmem_limit_bytes=32 * 1024 * 1024
        ),
    )(hyena, stream_in, feat_filter, inner_filter, queries, key_vectors, segments)

    tile = 2 * rows
    seg_lanes = segments.reshape(tokens // 128, 128)
    results = pl.pallas_call(
        functools.partial(attend_kernel, ring_z, tile),
        name="attend",
        out_shape=jax.ShapeDtypeStruct((ring_z, rows, HEAD_DIM), BF16),
        in_specs=[SMEM, VMEM, VMEM, VMEM, VMEM],
        out_specs=VMEM,
        scratch_shapes=[pltpu.VMEM((most // tile + 2, rows, tile), F32)],
        compiler_params=pltpu.CompilerParams(vmem_limit_bytes=32 * 1024 * 1024),
    )(segments, seg_lanes, q_all, k_all, v_all)

    attended = pl.pallas_call(
        functools.partial(return_kernel, ring_z),
        name="give_back",
        out_shape=jax.ShapeDtypeStruct((rows, channels), BF16),
        in_specs=[ANY],
        out_specs=ANY,
        scratch_shapes=[dma, dma((ring_z,)), dma((ring_z,))],
        compiler_params=pltpu.CompilerParams(collective_id=1, has_side_effects=True),
    )(results)
    return stream, attended


def solution(mesh):
    in_specs = (
        P("ctx", None, "tp"),
        P("ctx", "tp"),
        P(None, None, "tp"),
        P(None, "tp"),
        P("ctx", "tp"),
        P("ctx", "tp"),
        P(),
    )
    out_specs = (P("ctx", "tp"), P("ctx", "tp"))

    def whole(*args):
        most = args[-1].shape[0] // 2
        mapped = jax.shard_map(
            functools.partial(body, mesh.shape["ctx"], mesh.shape["tp"], most),
            mesh=mesh, in_specs=in_specs, out_specs=out_specs, check_vma=False,
        )
        return mapped(*args)

    return whole
```

time: 385 us -> 91.6 us (0.24)
  waiting for transfers between devices: 217 us -> 0 us
  Pallas kernels: 0 us -> 79.7 us
  local copies, waits for them, and re-layouts: 60.5 us -> 9.8 us
  other arithmetic: 36.8 us -> 0 us
  matrix products: 34.8 us -> 0 us
  between operations: 14.2 us -> 0.68 us
  blocking collectives: 10.7 us -> 0 us
  starting transfers between devices: 6.88 us -> 0 us
    all_gather x2 -> x0, waiting for transfers between devices: 215 us -> none  [the longest x1 119 us: body(): value_part = lax.all_gather(values, 'ctx', axis=0, tiled=True)]
    pallas_call x0 -> x3, Pallas kernels: none -> 79.7 us  [the longest x1 46.9 us: body(): pl.pallas_call(functools.partial(front_kernel, ring_z, ring_tp, rows), na...]
    dynamic_slice x49 -> x0, local copies, waits for them, and re-layouts: 43.7 us -> none  [the longest x24 27.1 us: block_turn(): value_block = lax.dynamic_slice_in_dim(value_part, block_start, 512)]
    dot_general x24 -> x0, matrix products: 34.8 us -> none  [the longest x12 21.9 us: fold_block(): jnp.einsum('qhd,khd->qhk', query_heads, key_heads, preferred_element_type...]
    and x12 -> x0, other arithmetic: 17 us -> none  [fold_block(): (seg_query[:, None] == seg_key[None, :]) & (key_pos[None, :] <= query_pos...]
    reduce_sum x13 -> x0, other arithmetic: 13.6 us -> none  [the longest x12 12.3 us: fold_block(): totals = totals * factor + jnp.sum(exp_terms, axis=2)]
    while x84 -> x0, local copies, waits for them, and re-layouts: 12.1 us -> none
    psum x1 -> x0, blocking collectives: 10.7 us -> none  [body(): row_total = lax.psum(jnp.sum(widened * widened, axis=1), 'tp')]
  transfers between devices with their start and end apart: 4 -> 0, of which waited for: 3 -> 0; matrix products, arithmetic and copies ran while one was open for 3% -> 0% of each run, Pallas kernels for 0% -> 0%
where the time goes in v1:
time: 91.6 us; the launch traced here: 90.1 us
  Pallas kernels  79.7 us (87%)
  local copies, waits for them, and re-layouts  9.8 us (11%)
    pallas_call x1, Pallas kernels, body(): pl.pallas_call(functools.partial(front_kernel, ring_z, ring_tp, rows), na...  46.9 us
    pallas_call x1, Pallas kernels, body(): pl.pallas_call(functools.partial(attend_kernel, ring_z, tile), name='atte...  18.7 us
    pallas_call x1, Pallas kernels, body(): pl.pallas_call(functools.partial(return_kernel, ring_z), name='give_back'...  14 us
    unnamed x18, local copies, waits for them, and re-layouts  9.8 us

profile of v1, /device:TPU:8, one launch (start us, length us, event | category | flops | bytes accessed | tf_op | source)
XLA Modules:
  0.0 90.1 jit_solution(4320176352898567115)
XLA Ops:
  0.6 0.0 copy-start.1
  0.6 1.3 %copy-done.1 = bf16[192,3,1024]{2,0,1:T(8,128)(2,1)S(1)} copy-done((bf16[192,3,1024]{2,0,1:T(8,128)(2,1)S(1)}, bf16[192,3,1024]{2,0,1:T(8,128)(2,1)}, u32[]{:S(2)}) %copy-start.1) | copy-done | bytes 1179672
  1.9 0.0 copy-start.2
  1.9 1.0 %copy-done.2 = bf16[192,1024]{1,0:T(8,128)(2,1)S(1)} copy-done((bf16[192,1024]{1,0:T(8,128)(2,1)S(1)}, bf16[192,1024]{1,0:T(8,128)(2,1)}, u32[]{:S(2)}) %copy-start.2) | copy-done | bytes 393240
  2.9 0.0 copy-start.3
  2.9 1.0 %copy-done.3 = bf16[192,1024]{1,0:T(8,128)(2,1)S(1)} copy-done((bf16[192,1024]{1,0:T(8,128)(2,1)S(1)}, bf16[192,1024]{1,0:T(8,128)(2,1)}, u32[]{:S(2)}) %copy-start.3) | copy-done | bytes 393240
  3.9 0.0 copy-start.4
  3.9 1.0 %copy-done.4 = bf16[192,1024]{1,0:T(8,128)(2,1)S(1)} copy-done((bf16[192,1024]{1,0:T(8,128)(2,1)S(1)}, bf16[192,1024]{1,0:T(8,128)(2,1)}, u32[]{:S(2)}) %copy-start.4) | copy-done | bytes 393240
  4.9 0.0 copy-start.5
  4.9 0.7 copy-done.5
  5.6 0.0 copy-start.6
  5.6 0.8 copy-done.6
  6.4 0.0 copy-start.7
  6.4 0.8 copy-done.7
  7.2 46.9 %front.1 = (bf16[192,1024]{1,0:T(8,128)(2,1)S(1)}, bf16[8,192,128]{2,1,0:T(8,128)(2,1)S(1)}, bf16[8,4,192,128]{3,2,1,0:T(8,128)(2,1)S(1)}, bf16[8,4,192,128]{3,2,1,0:T(8,128)(2,1)S(1)}) custom-call(bf16[3,192,1024]{2,1,0:T(8,128)(2,1)S(1)} %bitcast.2, bf16[192,1024]{1,0:T(8,128)(2,1)S(1)} %copy-done.2, f32[3,3,1024]{2,1,0:T(4,128)S(1)} %copy-done.6, ...), custom_call_target="tpu_custom_call" | custom-call | tf_op jit(solution)/shard_map/front/pallas_call | solution.py:434
  54.1 18.7 %attend.1.results = bf16[8,192,128]{2,1,0:T(8,128)(2,1)S(1)} custom-call(s32[6144]{0:T(1024)S(1)} %copy-done.5, s32[48,128]{1,0:T(8,128)S(1)} %bitcast.3, bf16[8,192,128]{2,1,0:T(8,128)(2,1)S(1)} %get-tuple-element.7.q_all, bf16[8,4,192,128]{3,2,1,0:T(8,128)(2,1)S(1)} %get-tuple-element.8.k_all, bf16[8,4,192,128]{3,2,1,0:T(8,128)(2,1)S(1)} %get-tuple-element.9.v_all), custom_call_target="tpu_custom_call" | custom-call | tf_op jit(solution)/shard_map/attend/pallas_call | solution.py:468
  72.8 0.0 copy-start
  72.8 0.7 copy-done
  73.6 14.0 %give_back.1 = bf16[192,1024]{1,0:T(8,128)(2,1)} custom-call(bf16[8,192,128]{2,1,0:T(8,128)(2,1)} %copy-done), custom_call_target="tpu_custom_call" | custom-call | tf_op jit(solution)/shard_map/give_back/pallas_call | solution.py:478
  87.6 0.7 copy.11
  88.4 1.8 %copy.12 = bf16[192,1024]{1,0:T(8,128)(2,1)} copy(bf16[192,1024]{1,0:T(8,128)(2,1)} %give_back.1) | data formatting | bytes 786432
Async XLA Ops:
  0.6 1.3 %copy-start.1 = (bf16[192,3,1024]{2,0,1:T(8,128)(2,1)S(1)}, bf16[192,3,1024]{2,0,1:T(8,128)(2,1)}, u32[]{:S(2)}) copy-start(bf16[192,3,1024]{2,0,1:T(8,128)(2,1)} %param.7) | copy-start | bytes 3538948
  1.9 1.0 %copy-start.2 = (bf16[192,1024]{1,0:T(8,128)(2,1)S(1)}, bf16[192,1024]{1,0:T(8,128)(2,1)}, u32[]{:S(2)}) copy-start(bf16[192,1024]{1,0:T(8,128)(2,1)} %stream_in.1) | copy-start | bytes 1179652
  2.9 1.0 %copy-start.3 = (bf16[192,1024]{1,0:T(8,128)(2,1)S(1)}, bf16[192,1024]{1,0:T(8,128)(2,1)}, u32[]{:S(2)}) copy-start(bf16[192,1024]{1,0:T(8,128)(2,1)} %queries.1) | copy-start | bytes 1179652
  3.9 1.0 %copy-start.4 = (bf16[192,1024]{1,0:T(8,128)(2,1)S(1)}, bf16[192,1024]{1,0:T(8,128)(2,1)}, u32[]{:S(2)}) copy-start(bf16[192,1024]{1,0:T(8,128)(2,1)} %keys.1) | copy-start | bytes 1179652
  4.9 0.7 copy-start.5
  5.6 0.8 copy-start.6
  6.4 0.8 copy-start.7
  72.8 0.7 copy-start

commit v2 on v1

v2 whole, which is shorter than its diff:
```python
import functools
import math

import jax
import jax.numpy as jnp
from jax import lax
from jax.experimental import pallas as pl
from jax.experimental.pallas import tpu as pltpu
from jax.sharding import PartitionSpec as P

HEAD_DIM = 128
HALO = 16
EPSILON = 1e-05
BIG = 1e30
CHUNK = 64
MESH = pl.DeviceIdType.MESH
F32 = jnp.float32
BF16 = jnp.bfloat16
RING_X = 4


def ring_offsets(count):
    offsets = [0]
    for distance in range(1, count // 2 + 1):
        offsets.append(distance)
        if distance != count - distance:
            offsets.append(-distance)
    return offsets


def slot_of(delta, count):
    ahead = jnp.maximum(2 * delta - 1, 0)
    return jnp.where(delta <= count // 2, ahead, 2 * (count - delta))


def mixer_kernel(
    ring_z, ring_tp, rows, most,
    hyena, stream_in, feat_in, inner_in, queries, keys, seg,
    stream_out, attended,
    hyena_buf, wide, product, gate_free, in_buf, stream_buf, values, feat, inner,
    seg_buf, turn_buf, seg_col, seg_query, sums, total_col,
    q_all, k_all, v_all, scores_buf, terms_buf, inverse, summed, results,
    load_sem, own_sem, halo_sem, sum_send, sum_recv,
    z_send, z_recv, x_send, x_recv, far_send, far_recv, back_send, back_recv,
):
    ctx = lax.axis_index("ctx")
    tp = lax.axis_index("tp")
    z = ctx // RING_X
    x = ctx % RING_X
    ring_ctx = ring_z * RING_X
    channels = queries.shape[1]
    offsets = ring_offsets(ring_z)
    half = rows // 2
    right = (x + 1) % RING_X
    left = (x + RING_X - 1) % RING_X
    far = (x + 2) % RING_X
    right_id = (z * RING_X + right, tp)
    left_id = (z * RING_X + left, tp)
    next_ctx = (ctx + 1) % ring_ctx
    prev_ctx = (ctx + ring_ctx - 1) % ring_ctx
    span = RING_X * rows
    reach = -(-most // span)
    lane_rows = span // 128
    turns = turn_buf.shape[0] // 128
    factor = math.log2(math.e) / math.sqrt(HEAD_DIM)

    def z_at(offset):
        return (z + offset + ring_z) % ring_z

    def head_cols(index):
        return pl.ds(pl.multiple_of(index * HEAD_DIM, HEAD_DIM), HEAD_DIM)

    loads = [
        pltpu.make_async_copy(source, target, load_sem.at[index])
        for index, (source, target) in enumerate((
            (seg, seg_buf),
            (feat_in, feat),
            (inner_in, inner),
            (hyena, hyena_buf.at[:, pl.ds(HALO, rows)]),
            (stream_in, in_buf),
        ))
    ]
    own_k = pltpu.make_async_copy(keys.at[:, head_cols(z)], k_all.at[0, x], own_sem.at[0])
    own_q = pltpu.make_async_copy(queries.at[:, head_cols(z)], q_all.at[0], own_sem.at[1])

    barrier = pltpu.get_barrier_semaphore()
    partners = [(z_at(offset) * RING_X + x, tp) for offset in offsets[1:]]
    partners += [right_id, left_id, (next_ctx, tp), (prev_ctx, tp)]
    partners += [(ctx, (tp + step) % ring_tp) for step in range(1, ring_tp)]
    for partner in partners:
        pl.semaphore_signal(barrier, inc=1, device_id=partner, device_id_type=MESH)
    for load in loads:
        load.start()
    own_k.start()
    own_q.start()

    def columns(block):
        first = block * rows
        top_row = first // 128 - 1
        for turn in range(turns):
            row = seg_buf[pl.ds(jnp.maximum(top_row + turn, 0), 1), :].astype(F32)
            turn_buf[pl.ds(turn * 128, 128), :] = jnp.broadcast_to(row, (128, 128)).T
        return pl.multiple_of(first - top_row * 128, 16)

    loads[0].wait()
    start_at = columns(ctx)
    seg_col[...] = turn_buf[pl.ds(start_at - HALO, HALO + rows), :]
    seg_col[pl.ds(0, HALO), :] = jnp.where(ctx == 0, -1.0, seg_col[pl.ds(0, HALO), :])
    seg_query[0] = seg_col[pl.ds(HALO, rows), :]

    pl.semaphore_wait(barrier, len(partners))

    halo = pltpu.make_async_remote_copy(
        src_ref=hyena.at[:, pl.ds(rows - HALO, HALO)],
        dst_ref=hyena_buf.at[:, pl.ds(0, HALO)],
        send_sem=halo_sem.at[0], recv_sem=halo_sem.at[1],
        device_id=(next_ctx, tp), device_id_type=MESH,
    )
    halo.start()

    def z_copy(kind, slot, source, target):
        goal = z_at(-offsets[slot])
        return pltpu.make_async_remote_copy(
            src_ref=source.at[:, head_cols(goal)], dst_ref=target,
            send_sem=z_send.at[kind, slot], recv_sem=z_recv.at[kind, slot],
            device_id=(goal * RING_X + x, tp), device_id_type=MESH,
        )

    k_copies = [z_copy(0, slot, keys, k_all.at[slot, x]) for slot in range(1, ring_z)]
    for copy in k_copies:
        copy.start()
    v_copies = [z_copy(1, slot, values, v_all.at[slot, x]) for slot in range(1, ring_z)]
    own_v = pltpu.make_async_copy(values.at[:, head_cols(z)], v_all.at[0, x], own_sem.at[2])
    q_copies = [z_copy(2, slot, queries, q_all.at[slot]) for slot in range(1, ring_z)]

    groups = [(0, 1)] + [(lo, min(lo + 2, ring_z)) for lo in range(1, ring_z, 2)]
    last_group = len(groups) - 1
    x_copies = []

    def near(kind, group, way, array, source):
        lo, hi = groups[group]
        view = array.at[pl.ds(lo, hi - lo), source]
        return pltpu.make_async_remote_copy(
            src_ref=view, dst_ref=view,
            send_sem=x_send.at[kind, group, way], recv_sem=x_recv.at[kind, group, way],
            device_id=(right_id, left_id)[way], device_id_type=MESH,
        )

    def further(kind, group, way, array, source):
        lo, hi = groups[group]
        view = array.at[pl.ds(lo, hi - lo), source, pl.ds(way * half, half)]
        return pltpu.make_async_remote_copy(
            src_ref=view, dst_ref=view,
            send_sem=far_send.at[kind, group, way], recv_sem=far_recv.at[kind, group, way],
            device_id=(right_id, left_id)[way], device_id_type=MESH,
        )

    def first_hop(kind, group):
        array, copies, own = ((k_all, k_copies, own_k), (v_all, v_copies, own_v))[kind]
        lo, hi = groups[group]
        if lo == 0:
            own.wait()
        else:
            for slot in range(lo, hi):
                copies[slot - 1].wait_recv()
        for way in range(2):
            copy = near(kind, group, way, array, x)
            copy.start()
            x_copies.append(copy)

    def second_hop(kind, group):
        array = (k_all, v_all)[kind]
        for way in range(2):
            near(kind, group, way, array, (left, right)[way]).wait_recv()
            copy = further(kind, group, way, array, (left, right)[way])
            copy.start()
            x_copies.append(copy)

    def arrived(kind):
        for group in range(len(groups)):
            for way in range(2):
                further(kind, group, way, (k_all, v_all)[kind], far).wait_recv()

    first_hop(0, 0)

    for load in loads[1:]:
        load.wait()
    wide[:, pl.ds(HALO, rows)] = hyena_buf[:, pl.ds(HALO, rows)].astype(F32)
    halo.wait_recv()
    wide[:, pl.ds(0, HALO)] = hyena_buf[:, pl.ds(0, HALO)].astype(F32)
    feat_taps, inner_taps = feat.shape[0], inner.shape[0]

    def tile_lanes(mask):
        return jnp.concatenate([mask] * (channels // 128), axis=1)

    def featured(group, start, count, masks):
        result = None
        for tap in range(feat_taps):
            term = feat[tap, group][None, :] * wide[group, pl.ds(start - tap, count), :]
            if tap > 0:
                term = term * masks[tap]
            result = term if result is None else result + term
        return result

    def masks_of(start, count, taps):
        here = seg_col[pl.ds(start, count), :]
        return [None] + [
            tile_lanes((seg_col[pl.ds(start - tap, count), :] == here).astype(F32))
            for tap in range(1, taps)
        ]

    masks = masks_of(8, 8, feat_taps)
    product[pl.ds(8, 8), :] = featured(1, 8, 8, masks) * featured(2, 8, 8, masks)

    relays = [functools.partial(first_hop, 0, group) for group in range(1, last_group)]
    between = rows // 8 // (len(relays) + 1) if relays else rows
    for step, start in enumerate(range(HALO, HALO + rows, 8)):
        if step > 0 and step % between == 0 and relays:
            relays.pop(0)()
        masks = masks_of(start, 8, inner_taps)
        key_value = featured(1, start, 8, masks) * featured(2, start, 8, masks)
        product[pl.ds(start, 8), :] = key_value
        mixing = inner[0][None, :] * key_value
        for tap in range(1, inner_taps):
            mixing = mixing + inner[tap][None, :] * product[pl.ds(start - tap, 8), :] * masks[tap]
        gate_free[pl.ds(start - HALO, 8), :] = featured(0, start, 8, masks) * mixing

    for start in range(0, rows, 16):
        stream = (in_buf[pl.ds(start, 16), :].astype(F32) + gate_free[pl.ds(start, 16), :]).astype(BF16)
        stream_buf[pl.ds(start, 16), :] = stream
        stream = stream.astype(F32)
        square = stream * stream
        folded = square[:, 0:128]
        for lane in range(128, channels, 128):
            folded = folded + square[:, lane:lane + 128]
        total_col[pl.ds(start, 16), :] = folded
    store_s = pltpu.make_async_copy(stream_buf, stream_out, load_sem.at[0])
    store_s.start()

    padded = total_col.shape[0]
    if padded > rows:
        total_col[pl.ds(rows, padded - rows), :] = jnp.zeros((padded - rows, 128), F32)
    for start in range(0, padded, 128):
        turned = total_col[pl.ds(start, 128), :].T
        row = jnp.sum(turned, axis=0, keepdims=True)
        sums[tp, :, pl.ds(start, 128)] = jnp.broadcast_to(row, (8, 128))
    sum_copies = []
    for step in range(1, ring_tp):
        copy = pltpu.make_async_remote_copy(
            src_ref=sums.at[tp], dst_ref=sums.at[tp],
            send_sem=sum_send.at[step], recv_sem=sum_recv.at[step],
            device_id=(ctx, (tp + step) % ring_tp), device_id_type=MESH,
        )
        copy.start()
        sum_copies.append(copy)
    early = min(4, ring_z - 1)
    for copy in q_copies[:early]:
        copy.start()

    total = sums[tp]
    for copy in sum_copies:
        copy.wait_recv()
    for step in range(1, ring_tp):
        total = total + sums[(tp + step) % ring_tp]
    scale = lax.rsqrt(total / (channels * ring_tp) + EPSILON)
    for start in range(0, padded, 128):
        row = jnp.broadcast_to(scale[0:1, start:start + 128], (128, 128))
        total_col[pl.ds(start, 128), :] = row.T
    for start in range(0, rows, 16):
        norm = tile_lanes(total_col[pl.ds(start, 16), :])
        values[pl.ds(start, 16), :] = (stream_buf[pl.ds(start, 16), :].astype(F32) * norm).astype(BF16)

    for copy in v_copies:
        copy.start()
    own_v.start()
    if last_group > 0:
        first_hop(0, last_group)
    for group in range(len(groups)):
        second_hop(0, group)
    first_hop(1, 0)

    def query_columns(slot, carry):
        row_z = (z + jnp.where(slot % 2 == 1, (slot + 1) // 2, ring_z - slot // 2)) % ring_z
        begin = columns(row_z * RING_X + x)
        seg_query[slot] = turn_buf[pl.ds(begin, rows), :]
        return carry

    lax.fori_loop(1, ring_z, query_columns, 0)
    for copy in q_copies[early:]:
        copy.start()
    arrived(0)

    def tile_of(array, row_z):
        slot = slot_of((row_z - z + ring_z) % ring_z, ring_z)
        return array[slot].reshape(span, HEAD_DIM)

    def weigh(slot):
        row_z = z_at(offsets[slot])
        low = jnp.maximum(row_z - reach, 0)

        def score(index, carry):
            scores_buf[index - low] = lax.dot_general(
                q_all[slot], tile_of(k_all, index), (((1,), (1,)), ((), ())),
                preferred_element_type=F32,
            )
            return carry

        lax.fori_loop(low, row_z + 1, score, 0)

        def mask_tile(index, top, diagonal):
            documents = jnp.concatenate(
                [seg_buf[pl.ds(index * lane_rows + i, 1), :] for i in range(lane_rows)], axis=1
            ).astype(F32)
            tops = []
            for start in range(0, rows, CHUNK):
                here = jnp.concatenate([seg_query[slot, pl.ds(start, CHUNK), :]] * lane_rows, axis=1)
                allowed = here == documents
                if diagonal:
                    row_at = x * rows + start + lax.broadcasted_iota(jnp.int32, (CHUNK, span), 0)
                    allowed = allowed & (lax.broadcasted_iota(jnp.int32, (CHUNK, span), 1) <= row_at)
                scores = jnp.where(allowed, scores_buf[index - low, pl.ds(start, CHUNK), :], -BIG)
                scores_buf[index - low, pl.ds(start, CHUNK), :] = scores
                most_here = top[start:start + CHUNK]
                for lane in range(0, span, 128):
                    most_here = jnp.maximum(most_here, scores[:, lane:lane + 128])
                tops.append(most_here)
            return jnp.concatenate(tops, axis=0)

        top = lax.fori_loop(
            low, row_z, lambda index, top: mask_tile(index, top, False), jnp.full((rows, 128), -BIG, F32)
        )
        top = mask_tile(row_z, top, True)
        top = jnp.broadcast_to(jnp.max(top, axis=1, keepdims=True), (rows, 128))

        def term_tile(index, totals):
            parts = []
            for start in range(0, rows, CHUNK):
                total_here = totals[start:start + CHUNK]
                for lane in range(0, span, 128):
                    scores = scores_buf[index - low, pl.ds(start, CHUNK), lane:lane + 128]
                    terms = jnp.exp2((scores - top[start:start + CHUNK]) * factor)
                    total_here = total_here + terms
                    terms_buf[slot, index - low, pl.ds(start, CHUNK), lane:lane + 128] = terms.astype(BF16)
                parts.append(total_here)
            return jnp.concatenate(parts, axis=0)

        totals = lax.fori_loop(low, row_z + 1, term_tile, jnp.zeros((rows, 128), F32))
        inverse[slot] = jnp.broadcast_to(1.0 / jnp.sum(totals, axis=1, keepdims=True), (rows, 128))

    def add_up(slot):
        row_z = z_at(offsets[slot])
        low = jnp.maximum(row_z - reach, 0)
        summed[...] = jnp.zeros((rows, HEAD_DIM), F32)

        def add_tile(index, carry):
            summed[...] += jnp.dot(
                terms_buf[slot, index - low], tile_of(v_all, index), preferred_element_type=F32
            )
            return carry

        lax.fori_loop(low, row_z + 1, add_tile, 0)
        results[slot] = (summed[...] * inverse[slot]).astype(BF16)

    back_copies = []

    def give_back(slot):
        copy = pltpu.make_async_remote_copy(
            src_ref=results.at[slot], dst_ref=attended.at[:, head_cols(z)],
            send_sem=back_send.at[slot], recv_sem=back_recv.at[slot],
            device_id=(z_at(offsets[slot]) * RING_X + x, tp), device_id_type=MESH,
        )
        copy.start()
        back_copies.append(copy)

    relays = [functools.partial(first_hop, 1, group) for group in range(1, len(groups))]
    relays += [functools.partial(second_hop, 1, group) for group in range(len(groups))]
    own_q.wait()
    for slot in range(early + 1):
        if slot > 0:
            q_copies[slot - 1].wait_recv()
        weigh(slot)
        for _ in range(2):
            if relays:
                relays.pop(0)()
    for relay in relays:
        relay()
    for slot in range(early + 1, ring_z):
        q_copies[slot - 1].wait_recv()
        weigh(slot)
    arrived(1)
    for slot in list(range(1, ring_z)) + [0]:
        add_up(slot)
        if slot > 0:
            give_back(slot)
    own_o = pltpu.make_async_copy(results.at[0], attended.at[:, head_cols(z)], own_sem.at[0])
    own_o.start()
    own_o.wait()
    for slot in range(1, ring_z):
        pltpu.make_async_remote_copy(
            src_ref=results.at[slot], dst_ref=attended.at[:, head_cols(z_at(-offsets[slot]))],
            send_sem=back_send.at[slot], recv_sem=back_recv.at[slot],
            device_id=(z_at(offsets[slot]) * RING_X + x, tp), device_id_type=MESH,
        ).wait_recv()
    store_s.wait()
    halo.wait_send()
    for copy in sum_copies + k_copies + v_copies + q_copies + x_copies + back_copies:
        copy.wait_send()


ANY = pl.BlockSpec(memory_space=pl.ANY)
HBM = pl.BlockSpec(memory_space=pltpu.HBM)


def body(ring_ctx, ring_tp, most, hyena_in, stream_in, feat_filter, inner_filter, queries, key_vectors, segments):
    rows, channels = stream_in.shape
    ring_z = ring_ctx // RING_X
    tokens = segments.shape[0]
    hyena = jnp.transpose(hyena_in, (1, 0, 2))
    padded = -(-rows // 128) * 128
    span = RING_X * rows
    tiles = -(-most // span) + 1
    groups = 1 + ring_z // 2
    turned = 128 * (-(-rows // 128) + 1)
    dma = pltpu.SemaphoreType.DMA
    block = pltpu.VMEM((rows, channels), BF16)
    gathered = pltpu.VMEM((ring_z, RING_X, rows, HEAD_DIM), BF16)
    by_row = (ring_z, rows, HEAD_DIM)
    out = jax.ShapeDtypeStruct((rows, channels), BF16)
    return pl.pallas_call(
        functools.partial(mixer_kernel, ring_z, ring_tp, rows, most),
        name="mixer",
        out_shape=(out, out),
        in_specs=[HBM] * 7,
        out_specs=(ANY, ANY),
        scratch_shapes=[
            pltpu.VMEM((3, HALO + rows, channels), BF16),
            pltpu.VMEM((3, HALO + rows, channels), F32),
            pltpu.VMEM((HALO + rows, channels), F32),
            pltpu.VMEM((rows, channels), F32),
            block, block, block,
            pltpu.VMEM(feat_filter.shape, F32),
            pltpu.VMEM(inner_filter.shape, F32),
            pltpu.VMEM((tokens // 128, 128), jnp.int32),
            pltpu.VMEM((turned, 128), F32),
            pltpu.VMEM((HALO + rows, 128), F32),
            pltpu.VMEM((ring_z, rows, 128), F32),
            pltpu.VMEM((ring_tp, 8, padded), F32),
            pltpu.VMEM((padded, 128), F32),
            pltpu.VMEM(by_row, BF16),
            gathered, gathered,
            pltpu.VMEM((tiles, rows, span), F32),
            pltpu.VMEM((ring_z, tiles, rows, span), BF16),
            pltpu.VMEM(by_row, F32),
            pltpu.VMEM((rows, HEAD_DIM), F32),
            pltpu.VMEM(by_row, BF16),
            dma((5,)), dma((3,)), dma((2,)), dma((ring_tp,)), dma((ring_tp,)),
            dma((3, ring_z)), dma((3, ring_z)),
            dma((2, groups, 2)), dma((2, groups, 2)),
            dma((2, groups, 2)), dma((2, groups, 2)),
            dma((ring_z,)), dma((ring_z,)),
        ],
        compiler_params=pltpu.CompilerParams(
            collective_id=0, has_side_effects=True, vmem_limit_bytes=48 * 1024 * 1024
        ),
    )(*(
        pltpu.with_memory_space_constraint(value, pltpu.HBM)
        for value in (
            hyena, stream_in, feat_filter, inner_filter, queries, key_vectors,
            segments.reshape(tokens // 128, 128),
        )
    ))


def solution(mesh):
    in_specs = (
        P("ctx", None, "tp"),
        P("ctx", "tp"),
        P(None, None, "tp"),
        P(None, "tp"),
        P("ctx", "tp"),
        P("ctx", "tp"),
        P(),
    )
    out_specs = (P("ctx", "tp"), P("ctx", "tp"))

    def whole(*args):
        most = args[-1].shape[0] // 2
        mapped = jax.shard_map(
            functools.partial(body, mesh.shape["ctx"], mesh.shape["tp"], most),
            mesh=mesh, in_specs=in_specs, out_specs=out_specs, check_vma=False,
        )
        return mapped(*args)

    return whole
```

time: 91.6 us -> 70.1 us (0.77)
  Pallas kernels: 79.7 us -> 67.1 us
  local copies, waits for them, and re-layouts: 9.8 us -> 1.49 us
    pallas_call x3 -> x1, Pallas kernels: 79.7 us -> 67.1 us  [body(): pl.pallas_call(functools.partial(mixer_kernel, ring_z, ring_tp, rows, mos...]
    unnamed x18 -> x2, local copies, waits for them, and re-layouts: 9.8 us -> 1.49 us
where the time goes in v2:
time: 70.1 us; the launch traced here: 69.2 us
  Pallas kernels  67.1 us (96%)
  local copies, waits for them, and re-layouts  1.49 us (2%)
    pallas_call x1, Pallas kernels, body(): pl.pallas_call(functools.partial(mixer_kernel, ring_z, ring_tp, rows, mos...  67.1 us
    unnamed x2, local copies, waits for them, and re-layouts  1.49 us

profile of v2, /device:TPU:8, one launch (start us, length us, event | category | flops | bytes accessed | tf_op | source)
XLA Modules:
  0.0 69.2 jit_solution(8075547069401329486)
XLA Ops:
  0.6 67.1 %mixer.1 = (bf16[192,1024]{1,0:T(8,128)(2,1)S(1)}, bf16[192,1024]{1,0:T(8,128)(2,1)S(1)}) custom-call(bf16[3,192,1024]{2,1,0:T(8,128)(2,1)} %bitcast.2, bf16[192,1024]{1,0:T(8,128)(2,1)} %stream_in.1, f32[3,3,1024]{2,1,0:T(4,128)} %feat_in.1, f32[7,1024]{1,0:T(8,128)} %inner_in.1, bf16[192,1024]{1,0:T(8,128)(2,1)} %queries.1, bf16[192,1024]{1,0:T(8,128)(2,1)} %keys.1, ...), custom_call_target="tpu_custom_call" | custom-call | tf_op jit(solution)/shard_map/mixer/pallas_call | solution.py:429
  67.7 0.7 %copy.11 = bf16[192,1024]{1,0:T(8,128)(2,1)} copy(bf16[192,1024]{1,0:T(8,128)(2,1)S(1)} %get-tuple-element.4) | data formatting | bytes 786432
  68.5 0.7 %copy.12 = bf16[192,1024]{1,0:T(8,128)(2,1)} copy(bf16[192,1024]{1,0:T(8,128)(2,1)S(1)} %get-tuple-element.5) | data formatting | bytes 786432

commit v3 on v2

--- a/solution.py
+++ b/solution.py
@@ -13,6 +13,10 @@
 EPSILON = 1e-05
 BIG = 1e30
 CHUNK = 64
+PRE_STEPS = 4
+EARLY = 2
+K_PUMPS = 3
+V_PUMPS = (1, 1, 2, 2, 2, 2)
 MESH = pl.DeviceIdType.MESH
 F32 = jnp.float32
 BF16 = jnp.bfloat16
@@ -39,7 +43,7 @@
     stream_out, attended,
     hyena_buf, wide, product, gate_free, in_buf, stream_buf, values, feat, inner,
     seg_buf, turn_buf, seg_col, seg_query, sums, total_col,
-    q_all, k_all, v_all, scores_buf, terms_buf, inverse, summed, results,
+    q_all, k_all, v_all, scores_buf, terms_buf, inverse, top_buf, summed, results,
     load_sem, own_sem, halo_sem, sum_send, sum_recv,
     z_send, z_recv, x_send, x_recv, far_send, far_recv, back_send, back_recv,
 ):
@@ -108,6 +112,49 @@
     seg_col[pl.ds(0, HALO), :] = jnp.where(ctx == 0, -1.0, seg_col[pl.ds(0, HALO), :])
     seg_query[0] = seg_col[pl.ds(HALO, rows), :]
 
+    feat_taps, inner_taps = feat.shape[0], inner.shape[0]
+
+    def tile_lanes(mask):
+        return jnp.concatenate([mask] * (channels // 128), axis=1)
+
+    def featured(group, start, count, masks):
+        result = None
+        for tap in range(feat_taps):
+            term = feat[tap, group][None, :] * wide[group, pl.ds(start - tap, count), :]
+            if tap > 0:
+                term = term * masks[tap]
+            result = term if result is None else result + term
+        return result
+
+    def masks_of(start, count, taps):
+        here = seg_col[pl.ds(start, count), :]
+        return [None] + [
+            tile_lanes((seg_col[pl.ds(start - tap, count), :] == here).astype(F32))
+            for tap in range(1, taps)
+        ]
+
+    def product_only(start):
+        masks = masks_of(start, 8, feat_taps)
+        product[pl.ds(start, 8), :] = featured(1, start, 8, masks) * featured(2, start, 8, masks)
+
+    def convolve(start):
+        masks = masks_of(start, 8, inner_taps)
+        key_value = featured(1, start, 8, masks) * featured(2, start, 8, masks)
+        product[pl.ds(start, 8), :] = key_value
+        mixing = inner[0][None, :] * key_value
+        for tap in range(1, inner_taps):
+            mixing = mixing + inner[tap][None, :] * product[pl.ds(start - tap, 8), :] * masks[tap]
+        gate_free[pl.ds(start - HALO, 8), :] = featured(0, start, 8, masks) * mixing
+
+    inside = list(range(HALO + 16, HALO + rows, 8))
+    before = min(PRE_STEPS, len(inside))
+    for load in loads[1:]:
+        load.wait()
+    wide[:, pl.ds(HALO, rows)] = hyena_buf[:, pl.ds(HALO, rows)].astype(F32)
+    product_only(HALO + 8)
+    for start in inside[:before]:
+        convolve(start)
+
     pl.semaphore_wait(barrier, len(partners))
 
     halo = pltpu.make_async_remote_copy(
@@ -183,48 +230,20 @@
 
     first_hop(0, 0)
 
-    for load in loads[1:]:
-        load.wait()
-    wide[:, pl.ds(HALO, rows)] = hyena_buf[:, pl.ds(HALO, rows)].astype(F32)
+    for start in inside[before:]:
+        convolve(start)
+    waiting = [functools.partial(first_hop, 0, group) for group in range(1, len(groups))]
+
+    def pump(count):
+        for _ in range(min(count, len(waiting))):
+            waiting.pop(0)()
+
+    pump(1)
     halo.wait_recv()
     wide[:, pl.ds(0, HALO)] = hyena_buf[:, pl.ds(0, HALO)].astype(F32)
-    feat_taps, inner_taps = feat.shape[0], inner.shape[0]
-
-    def tile_lanes(mask):
-        return jnp.concatenate([mask] * (channels // 128), axis=1)
-
-    def featured(group, start, count, masks):
-        result = None
-        for tap in range(feat_taps):
-            term = feat[tap, group][None, :] * wide[group, pl.ds(start - tap, count), :]
-            if tap > 0:
-                term = term * masks[tap]
-            result = term if result is None else result + term
-        return result
-
-    def masks_of(start, count, taps):
-        here = seg_col[pl.ds(start, count), :]
-        return [None] + [
-            tile_lanes((seg_col[pl.ds(start - tap, count), :] == here).astype(F32))
-            for tap in range(1, taps)
-        ]
-
-    masks = masks_of(8, 8, feat_taps)
-    product[pl.ds(8, 8), :] = featured(1, 8, 8, masks) * featured(2, 8, 8, masks)
-
-    relays = [functools.partial(first_hop, 0, group) for group in range(1, last_group)]
-    between = rows // 8 // (len(relays) + 1) if relays else rows
-    for step, start in enumerate(range(HALO, HALO + rows, 8)):
-        if step > 0 and step % between == 0 and relays:
-            relays.pop(0)()
-        masks = masks_of(start, 8, inner_taps)
-        key_value = featured(1, start, 8, masks) * featured(2, start, 8, masks)
-        product[pl.ds(start, 8), :] = key_value
-        mixing = inner[0][None, :] * key_value
-        for tap in range(1, inner_taps):
-            mixing = mixing + inner[tap][None, :] * product[pl.ds(start - tap, 8), :] * masks[tap]
-        gate_free[pl.ds(start - HALO, 8), :] = featured(0, start, 8, masks) * mixing
-
+    product_only(8)
+    convolve(HALO)
+    convolve(HALO + 8)
     for start in range(0, rows, 16):
         stream = (in_buf[pl.ds(start, 16), :].astype(F32) + gate_free[pl.ds(start, 16), :]).astype(BF16)
         stream_buf[pl.ds(start, 16), :] = stream
@@ -253,10 +272,13 @@
         )
         copy.start()
         sum_copies.append(copy)
-    early = min(4, ring_z - 1)
+    early = min(EARLY, ring_z - 1)
     for copy in q_copies[:early]:
         copy.start()
 
+    waiting[1:1] = [functools.partial(second_hop, 0, 0)]
+    waiting[3:3] = [functools.partial(second_hop, 0, 1)]
+    pump(K_PUMPS)
     total = sums[tp]
     for copy in sum_copies:
         copy.wait_recv()
@@ -273,11 +295,11 @@
     for copy in v_copies:
         copy.start()
     own_v.start()
-    if last_group > 0:
-        first_hop(0, last_group)
-    for group in range(len(groups)):
-        second_hop(0, group)
-    first_hop(1, 0)
+    for copy in q_copies[early:]:
+        copy.start()
+    waiting += [functools.partial(second_hop, 0, group) for group in range(2, len(groups))]
+    waiting += [functools.partial(first_hop, 1, 0)]
+    pump(len(waiting))
 
     def query_columns(slot, carry):
         row_z = (z + jnp.where(slot % 2 == 1, (slot + 1) // 2, ring_z - slot // 2)) % ring_z
@@ -286,8 +308,9 @@
         return carry
 
     lax.fori_loop(1, ring_z, query_columns, 0)
-    for copy in q_copies[early:]:
-        copy.start()
+    waiting += [functools.partial(first_hop, 1, group) for group in range(1, len(groups))]
+    waiting += [functools.partial(second_hop, 1, group) for group in range(len(groups))]
+    pump(1)
     arrived(0)
 
     def tile_of(array, row_z):
@@ -305,7 +328,14 @@
             )
             return carry
 
-        lax.fori_loop(low, row_z + 1, score, 0)
+        @pl.when(row_z < reach)
+        def _():
+            lax.fori_loop(0, row_z + 1, score, 0)
+
+        @pl.when(row_z >= reach)
+        def _():
+            for index in range(reach + 1):
+                score(low + index, 0)
 
         def mask_tile(index, top, diagonal):
             documents = jnp.concatenate(
@@ -326,31 +356,54 @@
                 tops.append(most_here)
             return jnp.concatenate(tops, axis=0)
 
-        top = lax.fori_loop(
-            low, row_z, lambda index, top: mask_tile(index, top, False), jnp.full((rows, 128), -BIG, F32)
-        )
-        top = mask_tile(row_z, top, True)
-        top = jnp.broadcast_to(jnp.max(top, axis=1, keepdims=True), (rows, 128))
+        def largest(top):
+            top = mask_tile(row_z, top, True)
+            top_buf[...] = jnp.broadcast_to(jnp.max(top, axis=1, keepdims=True), (rows, 128))
+
+        @pl.when(row_z < reach)
+        def _():
+            largest(lax.fori_loop(
+                0, row_z, lambda index, top: mask_tile(index, top, False),
+                jnp.full((rows, 128), -BIG, F32),
+            ))
+
+        @pl.when(row_z >= reach)
+        def _():
+            top = jnp.full((rows, 128), -BIG, F32)
+            for index in range(reach):
+                top = mask_tile(low + index, top, False)
+            largest(top)
 
         def term_tile(index, totals):
             parts = []
             for start in range(0, rows, CHUNK):
                 total_here = totals[start:start + CHUNK]
+                top = top_buf[pl.ds(start, CHUNK), :]
                 for lane in range(0, span, 128):
-                    scores = scores_buf[index - low, pl.ds(start, CHUNK), lane:lane + 128]
-                    terms = jnp.exp2((scores - top[start:start + CHUNK]) * factor)
+                    scores = scores_buf[index, pl.ds(start, CHUNK), lane:lane + 128]
+                    terms = jnp.exp2((scores - top) * factor)
                     total_here = total_here + terms
-                    terms_buf[slot, index - low, pl.ds(start, CHUNK), lane:lane + 128] = terms.astype(BF16)
+                    terms_buf[slot, index, pl.ds(start, CHUNK), lane:lane + 128] = terms.astype(BF16)
                 parts.append(total_here)
             return jnp.concatenate(parts, axis=0)
 
-        totals = lax.fori_loop(low, row_z + 1, term_tile, jnp.zeros((rows, 128), F32))
-        inverse[slot] = jnp.broadcast_to(1.0 / jnp.sum(totals, axis=1, keepdims=True), (rows, 128))
+        def divide_by(totals):
+            inverse[slot] = jnp.broadcast_to(1.0 / jnp.sum(totals, axis=1, keepdims=True), (rows, 128))
+
+        @pl.when(row_z < reach)
+        def _():
+            divide_by(lax.fori_loop(0, row_z + 1, term_tile, jnp.zeros((rows, 128), F32)))
+
+        @pl.when(row_z >= reach)
+        def _():
+            totals = jnp.zeros((rows, 128), F32)
+            for index in range(reach + 1):
+                totals = term_tile(index, totals)
+            divide_by(totals)
 
     def add_up(slot):
         row_z = z_at(offsets[slot])
         low = jnp.maximum(row_z - reach, 0)
-        summed[...] = jnp.zeros((rows, HEAD_DIM), F32)
 
         def add_tile(index, carry):
             summed[...] += jnp.dot(
@@ -358,7 +411,21 @@
             )
             return carry
 
-        lax.fori_loop(low, row_z + 1, add_tile, 0)
+        @pl.when(row_z < reach)
+        def _():
+            summed[...] = jnp.zeros((rows, HEAD_DIM), F32)
+            lax.fori_loop(0, row_z + 1, add_tile, 0)
+
+        @pl.when(row_z >= reach)
+        def _():
+            total = None
+            for index in range(reach + 1):
+                part = jnp.dot(
+                    terms_buf[slot, index], tile_of(v_all, low + index), preferred_element_type=F32
+                )
+                total = part if total is None else total + part
+            summed[...] = total
+
         results[slot] = (summed[...] * inverse[slot]).astype(BF16)
 
     back_copies = []
@@ -372,23 +439,15 @@
         copy.start()
         back_copies.append(copy)
 
-    relays = [functools.partial(first_hop, 1, group) for group in range(1, len(groups))]
-    relays += [functools.partial(second_hop, 1, group) for group in range(len(groups))]
     own_q.wait()
-    for slot in range(early + 1):
+    for slot in range(ring_z):
         if slot > 0:
             q_copies[slot - 1].wait_recv()
         weigh(slot)
-        for _ in range(2):
-            if relays:
-                relays.pop(0)()
-    for relay in relays:
-        relay()
-    for slot in range(early + 1, ring_z):
-        q_copies[slot - 1].wait_recv()
-        weigh(slot)
+        pump(V_PUMPS[slot] if slot < len(V_PUMPS) else 0)
+    pump(len(waiting))
     arrived(1)
-    for slot in list(range(1, ring_z)) + [0]:
+    for slot in reversed(range(ring_z)):
         add_up(slot)
         if slot > 0:
             give_back(slot)
@@ -451,6 +510,7 @@
             pltpu.VMEM((tiles, rows, span), F32),
             pltpu.VMEM((ring_z, tiles, rows, span), BF16),
             pltpu.VMEM(by_row, F32),
+            pltpu.VMEM((rows, 128), F32),
             pltpu.VMEM((rows, HEAD_DIM), F32),
             pltpu.VMEM(by_row, BF16),
             dma((5,)), dma((3,)), dma((2,)), dma((ring_tp,)), dma((ring_tp,)),

time: 70.1 us -> 59.3 us (0.85)
  Pallas kernels: 67.1 us -> 56.1 us
    pallas_call x1, Pallas kernels: 67.1 us -> 56.1 us  [body(): pl.pallas_call(functools.partial(mixer_kernel, ring_z, ring_tp, rows, mos...]
where the time goes in v3:
time: 59.3 us; the launch traced here: 58.2 us
  Pallas kernels  56.1 us (95%)
  local copies, waits for them, and re-layouts  1.49 us (3%)
  between operations  0.64 us (1%)
    pallas_call x1, Pallas kernels, body(): pl.pallas_call(functools.partial(mixer_kernel, ring_z, ring_tp, rows, mos...  56.1 us
    unnamed x2, local copies, waits for them, and re-layouts  1.49 us

profile of v3, /device:TPU:8, one launch (start us, length us, event | category | flops | bytes accessed | tf_op | source)
XLA Modules:
  0.0 58.2 jit_solution(17547135567553359937)
XLA Ops:
  0.6 56.1 %mixer.1 = (bf16[192,1024]{1,0:T(8,128)(2,1)S(1)}, bf16[192,1024]{1,0:T(8,128)(2,1)S(1)}) custom-call(bf16[3,192,1024]{2,1,0:T(8,128)(2,1)} %bitcast.2, bf16[192,1024]{1,0:T(8,128)(2,1)} %stream_in.1, f32[3,3,1024]{2,1,0:T(4,128)} %feat_in.1, f32[7,1024]{1,0:T(8,128)} %inner_in.1, bf16[192,1024]{1,0:T(8,128)(2,1)} %queries.1, bf16[192,1024]{1,0:T(8,128)(2,1)} %keys.1, ...), custom_call_target="tpu_custom_call" | custom-call | tf_op jit(solution)/shard_map/mixer/pallas_call | solution.py:488
  56.7 0.7 %copy.11 = bf16[192,1024]{1,0:T(8,128)(2,1)} copy(bf16[192,1024]{1,0:T(8,128)(2,1)S(1)} %get-tuple-element.4) | data formatting | bytes 786432
  57.5 0.7 %copy.12 = bf16[192,1024]{1,0:T(8,128)(2,1)} copy(bf16[192,1024]{1,0:T(8,128)(2,1)S(1)} %get-tuple-element.5) | data formatting | bytes 786432

commit v4 on v3

--- a/solution.py
+++ b/solution.py
@@ -16,7 +16,7 @@
 PRE_STEPS = 4
 EARLY = 2
 K_PUMPS = 3
-V_PUMPS = (1, 1, 2, 2, 2, 2)
+V_PUMPS = ((0, 1), (1, 1), (1, 1), (1, 1), (0, 1))
 MESH = pl.DeviceIdType.MESH
 F32 = jnp.float32
 BF16 = jnp.bfloat16
@@ -279,6 +279,14 @@
     waiting[1:1] = [functools.partial(second_hop, 0, 0)]
     waiting[3:3] = [functools.partial(second_hop, 0, 1)]
     pump(K_PUMPS)
+
+    def query_columns(slot, carry):
+        row_z = (z + jnp.where(slot % 2 == 1, (slot + 1) // 2, ring_z - slot // 2)) % ring_z
+        begin = columns(row_z * RING_X + x)
+        seg_query[slot] = turn_buf[pl.ds(begin, rows), :]
+        return carry
+
+    lax.fori_loop(1, ring_z, query_columns, 0)
     total = sums[tp]
     for copy in sum_copies:
         copy.wait_recv()
@@ -301,15 +309,11 @@
     waiting += [functools.partial(first_hop, 1, 0)]
     pump(len(waiting))
 
-    def query_columns(slot, carry):
-        row_z = (z + jnp.where(slot % 2 == 1, (slot + 1) // 2, ring_z - slot // 2)) % ring_z
-        begin = columns(row_z * RING_X + x)
-        seg_query[slot] = turn_buf[pl.ds(begin, rows), :]
-        return carry
-
-    lax.fori_loop(1, ring_z, query_columns, 0)
-    waiting += [functools.partial(first_hop, 1, group) for group in range(1, len(groups))]
-    waiting += [functools.partial(second_hop, 1, group) for group in range(len(groups))]
+    for group in range(1, len(groups) + 2):
+        if group < len(groups):
+            waiting.append(functools.partial(first_hop, 1, group))
+        if group >= 2:
+            waiting.append(functools.partial(second_hop, 1, group - 2))
     pump(1)
     arrived(0)
 
@@ -317,7 +321,7 @@
         slot = slot_of((row_z - z + ring_z) % ring_z, ring_z)
         return array[slot].reshape(span, HEAD_DIM)
 
-    def weigh(slot):
+    def weigh(slot, relays):
         row_z = z_at(offsets[slot])
         low = jnp.maximum(row_z - reach, 0)
 
@@ -336,6 +340,8 @@
         def _():
             for index in range(reach + 1):
                 score(low + index, 0)
+
+        pump(relays)
 
         def mask_tile(index, top, diagonal):
             documents = jnp.concatenate(
@@ -443,8 +449,9 @@
     for slot in range(ring_z):
         if slot > 0:
             q_copies[slot - 1].wait_recv()
-        weigh(slot)
-        pump(V_PUMPS[slot] if slot < len(V_PUMPS) else 0)
+        inside_it, after_it = V_PUMPS[slot] if slot < len(V_PUMPS) else (0, 0)
+        weigh(slot, inside_it)
+        pump(after_it)
     pump(len(waiting))
     arrived(1)
     for slot in reversed(range(ring_z)):
@@ -466,6 +473,17 @@
         copy.wait_send()
 
 
+def place_kernel(stream_from, attended_from, stream, attended, sem):
+    copies = [
+        pltpu.make_async_copy(stream_from, stream, sem.at[0]),
+        pltpu.make_async_copy(attended_from, attended, sem.at[1]),
+    ]
+    for copy in copies:
+        copy.start()
+    for copy in copies:
+        copy.wait()
+
+
 ANY = pl.BlockSpec(memory_space=pl.ANY)
 HBM = pl.BlockSpec(memory_space=pltpu.HBM)
 
@@ -485,7 +503,7 @@
     gathered = pltpu.VMEM((ring_z, RING_X, rows, HEAD_DIM), BF16)
     by_row = (ring_z, rows, HEAD_DIM)
     out = jax.ShapeDtypeStruct((rows, channels), BF16)
-    return pl.pallas_call(
+    results = pl.pallas_call(
         functools.partial(mixer_kernel, ring_z, ring_tp, rows, most),
         name="mixer",
         out_shape=(out, out),
@@ -529,6 +547,15 @@
             segments.reshape(tokens // 128, 128),
         )
     ))
+    return pl.pallas_call(
+        place_kernel,
+        name="place",
+        out_shape=(out, out),
+        in_specs=[ANY] * 2,
+        out_specs=(ANY, ANY),
+        scratch_shapes=[dma((2,))],
+        compiler_params=pltpu.CompilerParams(vmem_limit_bytes=48 * 1024 * 1024),
+    )(*results)
 
 
 def solution(mesh):

time: 59.3 us -> 58.5 us (0.987); the launches traced: 58.2 us -> 58.4 us
  local copies, waits for them, and re-layouts: 1.49 us -> 0 us
  Pallas kernels: 56.1 us -> 57.5 us
    unnamed x2 -> x0, local copies, waits for them, and re-layouts: 1.49 us -> none
    pallas_call x0 -> x1, Pallas kernels: none -> 0.89 us  [body(): pl.pallas_call(place_kernel, name='place', out_shape=(out, out), in_specs...]
where the time goes in v4:
time: 58.5 us; the launch traced here: 58.4 us
  Pallas kernels  57.5 us (98%)
  between operations  0.82 us (1%)
    pallas_call x1, Pallas kernels, body(): pl.pallas_call(functools.partial(mixer_kernel, ring_z, ring_tp, rows, mos...  56.6 us

profile of v4, /device:TPU:8, one launch (start us, length us, event | category | flops | bytes accessed | tf_op | source)
XLA Modules:
  0.0 58.4 jit_solution(10677976417287780747)
XLA Ops:
  0.6 56.6 %mixer.1 = (bf16[192,1024]{1,0:T(8,128)(2,1)S(1)}, bf16[192,1024]{1,0:T(8,128)(2,1)S(1)}) custom-call(bf16[3,192,1024]{2,1,0:T(8,128)(2,1)} %bitcast.2, bf16[192,1024]{1,0:T(8,128)(2,1)} %stream_in.1, f32[3,3,1024]{2,1,0:T(4,128)} %feat_in.1, f32[7,1024]{1,0:T(8,128)} %inner_in.1, bf16[192,1024]{1,0:T(8,128)(2,1)} %queries.1, bf16[192,1024]{1,0:T(8,128)(2,1)} %keys.1, ...), custom_call_target="tpu_custom_call" | custom-call | tf_op jit(solution)/shard_map/mixer/pallas_call | solution.py:506
  57.3 0.9 %place.1 = (bf16[192,1024]{1,0:T(8,128)(2,1)}, bf16[192,1024]{1,0:T(8,128)(2,1)}) custom-call(bf16[192,1024]{1,0:T(8,128)(2,1)S(1)} %get-tuple-element.4.stream_from, bf16[192,1024]{1,0:T(8,128)(2,1)S(1)} %get-tuple-element.5.attended_from), custom_call_target="tpu_custom_call" | custom-call | tf_op jit(solution)/shard_map/place/pallas_call | solution.py:550

commit v5 on v4

--- a/solution.py
+++ b/solution.py
@@ -15,7 +15,7 @@
 CHUNK = 64
 PRE_STEPS = 4
 EARLY = 2
-K_PUMPS = 3
+K_PUMPS = 2
 V_PUMPS = ((0, 1), (1, 1), (1, 1), (1, 1), (0, 1))
 MESH = pl.DeviceIdType.MESH
 F32 = jnp.float32

time: 58.5 us -> 59.2 us (1.012)
  Pallas kernels: 57.5 us -> 58.2 us
    pallas_call x1, Pallas kernels: 56.6 us -> 57.3 us  [body(): pl.pallas_call(functools.partial(mixer_kernel, ring_z, ring_tp, rows, mos...]
where the time goes in v5:
time: 59.2 us; the launch traced here: 59 us
  Pallas kernels  58.2 us (98%)
  between operations  0.82 us (1%)
    pallas_call x1, Pallas kernels, body(): pl.pallas_call(functools.partial(mixer_kernel, ring_z, ring_tp, rows, mos...  57.3 us

profile of v5, /device:TPU:8, one launch (start us, length us, event | category | flops | bytes accessed | tf_op | source)
XLA Modules:
  0.0 59.0 jit_solution(9863463806691113227)
XLA Ops:
  0.6 57.3 %mixer.1 = (bf16[192,1024]{1,0:T(8,128)(2,1)S(1)}, bf16[192,1024]{1,0:T(8,128)(2,1)S(1)}) custom-call(bf16[3,192,1024]{2,1,0:T(8,128)(2,1)} %bitcast.2, bf16[192,1024]{1,0:T(8,128)(2,1)} %stream_in.1, f32[3,3,1024]{2,1,0:T(4,128)} %feat_in.1, f32[7,1024]{1,0:T(8,128)} %inner_in.1, bf16[192,1024]{1,0:T(8,128)(2,1)} %queries.1, bf16[192,1024]{1,0:T(8,128)(2,1)} %keys.1, ...), custom_call_target="tpu_custom_call" | custom-call | tf_op jit(solution)/shard_map/mixer/pallas_call | solution.py:506
  58.0 0.9 %place.1 = (bf16[192,1024]{1,0:T(8,128)(2,1)}, bf16[192,1024]{1,0:T(8,128)(2,1)}) custom-call(bf16[192,1024]{1,0:T(8,128)(2,1)S(1)} %get-tuple-element.4.stream_from, bf16[192,1024]{1,0:T(8,128)(2,1)S(1)} %get-tuple-element.5.attended_from), custom_call_target="tpu_custom_call" | custom-call | tf_op jit(solution)/shard_map/place/pallas_call | solution.py:550
